TPU v7x, 32 devices: a whole 2x2x4 slice. The times are simulated.
32 devices in a mesh: gy: 4 (over z), gz: 8 (over y, x, core).
Axes of the slice: x: 2, y: 2, z: 4, core: 2. Of those that a mesh axis runs over, the one named last changes fastest.
Arguments:
- snapshots: float32 [16, 3, 1, 512, 512], P(None, None, None, 'gz', 'gy'), may hold values from -6 to 6
- cell_weight: float32 [512], P('gy'), may hold values from 0.4 to 7.5, as said below
Outputs:
- pod_modes: float32 [16, 3, 1, 512, 512], P(None, None, None, 'gz', 'gy')
- factor: float32 [16, 16], replicated
Inputs may be any that keep to these rules, and one draw needn't show every extreme that they name: `cell_weight`: weights are positive.
All inputs are finite; a program needn't handle non-finite values.
Results may differ from a plain program's by a relative error of at most 0.000071.
Values sent between devices are 32-bit elements; how exact they have to be, the bound alone decides.
A program may use at most 64 MiB of HBM per device.

v0:
```python
import math

import jax
import jax.numpy as jnp
from jax import lax
from jax.sharding import PartitionSpec as P

FILTER_RAW = [math.exp(-(offset - 4) * (offset - 4) / 4.5) for offset in range(9)]
FILTER_TAPS = [value / sum(FILTER_RAW) for value in FILTER_RAW]


def with_halo(block, sides, width, periodic):
    for axis, dim in sides:
        count = lax.axis_size(axis)
        forward = [(i, i + 1) for i in range(count - 1)]
        if periodic:
            forward.append((count - 1, 0))
        backward = [(target, source) for source, target in forward]
        low = lax.ppermute(
            lax.slice_in_dim(block, block.shape[dim] - width, None, axis=dim), axis, forward
        )
        high = lax.ppermute(lax.slice_in_dim(block, 0, width, axis=dim), axis, backward)
        block = jnp.concatenate([low, block, high], axis=dim)
    return block


def filter_axis(padded, length, axis_dim):
    return sum(
        (
            FILTER_TAPS[offset] * lax.slice_in_dim(padded, offset, offset + length, axis=axis_dim)
            for offset in range(9)
        )
    )


def per_device(snapshots, cell_weight):
    cells_z = snapshots.shape[3]
    cells_y = snapshots.shape[4]
    padded = with_halo(snapshots, (("gy", 4),), 4, False)
    smooth_y = filter_axis(padded, cells_y, 4)
    padded_z = with_halo(smooth_y, (("gz", 3),), 4, True)
    smooth = filter_axis(padded_z, cells_z, 3)
    weighted = smooth * jnp.sqrt(cell_weight)[None, None, None, None, :]
    flat_rows = weighted.reshape(weighted.shape[0], -1)
    gram_local = jnp.dot(
        flat_rows, flat_rows.T, precision=lax.Precision.HIGHEST, preferred_element_type=jnp.float32
    )
    summed_gram = lax.psum(gram_local, ("gy", "gz"))
    upper_factor = jnp.linalg.cholesky(summed_gram).T
    row_total = flat_rows.shape[1] * lax.axis_size("gy") * lax.axis_size("gz")
    basis_rows = lax.linalg.triangular_solve(upper_factor.T, flat_rows, left_side=True, lower=True)
    pod_modes = (basis_rows * math.sqrt(row_total)).reshape(weighted.shape)
    return (pod_modes, upper_factor / math.sqrt(row_total))


def solution(mesh):
    return jax.shard_map(
        per_device,
        mesh=mesh,
        in_specs=(P(None, None, None, "gz", "gy"), P("gy")),
        out_specs=(P(None, None, None, "gz", "gy"), P()),
        check_vma=False,
    )
```

profile of v0, /device:TPU:0, one launch (start us, length us, event | category | flops | bytes accessed | tf_op | source)
XLA Modules:
  0.0 86.0 jit_solution(11014285719047272861)
XLA Ops:
  0.6 2.5 %fusion.58 = (f32[16,3,1,64,4]{4,3,2,1,0:T(8,128)S(1)}, f32[16,3,1,64,4]{4,3,2,1,0:T(8,128)S(1)}) fusion(f32[16,3,1,64,128]{4,3,2,1,0:T(8,128)} %param.2), kind=kLoop, calls=%fused_computation.91 | loop fusion | bytes 196608 | tf_op jit(solution)/shard_map/slice | solution.py:20
  3.2 0.5 copy.22
  3.7 4.9 %collective-permute-start = (f32[16,3,1,64,4]{3,0,4,2,1:T(8,128)S(1)}, f32[16,3,1,64,4]{3,0,4,2,1:T(8,128)S(1)}, u32[]{:S(2)}, u32[]{:S(2)}) collective-permute-start(f32[16,3,1,64,4]{3,0,4,2,1:T(8,128)S(1)} %copy.22), channel_id=1, source_target_pairs={{0,8},{8,16},{16,24},{1,9},{9,17},{17,25},{2,10},{10,18},{18,26},{... | collective-permute-start | bytes 147464 | tf_op jit(solution)/shard_map/ppermute | solution.py:19
  8.6 0.5 copy.23
  9.1 0.0 copy-start
  9.2 1.4 %collective-permute-start.1 = (f32[16,3,1,64,4]{3,0,4,2,1:T(8,128)S(1)}, f32[16,3,1,64,4]{3,0,4,2,1:T(8,128)S(1)}, u32[]{:S(2)}, u32[]{:S(2)}) collective-permute-start(f32[16,3,1,64,4]{3,0,4,2,1:T(8,128)S(1)} %copy.23), channel_id=1, source_target_pairs={{8,0},{16,8},{24,16},{9,1},{17,9},{25,17},{10,2},{18,10},{26,18},{... | collective-permute-start | bytes 147464 | tf_op jit(solution)/shard_map/ppermute | solution.py:22
  10.6 0.2 collective-permute-done
  10.8 0.5 copy.11
  11.4 4.4 %collective-permute-done.1 = f32[16,3,1,64,4]{3,0,4,2,1:T(8,128)S(1)} collective-permute-done((f32[16,3,1,64,4]{3,0,4,2,1:T(8,128)S(1)}, f32[16,3,1,64,4]{3,0,4,2,1:T(8,128)S(1)}, u32[]{:S(2)}, u32[]{:S(2)}) %collective-permute-start.1) | collective-permute-done | bytes 49184 | tf_op jit(solution)/shard_map/ppermute | solution.py:22
  15.8 1.7 %copy.13 = f32[16,3,1,64,4]{4,3,2,1,0:T(8,128)} copy(f32[16,3,1,64,4]{3,0,4,2,1:T(8,128)S(1)} %collective-permute-done.1) | data formatting | bytes 98304 | tf_op jit(solution)/shard_map/ppermute | solution.py:22
  17.5 0.0 copy-done
  17.5 0.0 copy-start.1
  17.5 9.7 %fusion.24 = f32[16,3,1,64,128]{4,3,2,1,0:T(8,128)S(1)} fusion(f32[16,3,1,64,128]{4,3,2,1,0:T(8,128)S(1)} %copy-done, f32[16,3,1,64,4]{4,3,2,1,0:T(8,128)} %copy.13, f32[16,3,1,64,4]{4,3,2,1,0:T(8,128)S(1)} %copy.11), kind=kLoop, calls=%fused_computation.49 | loop fusion | flops 9830400 | bytes 3244032 | tf_op jit(solution)/shard_map/add | solution.py:28
  27.2 0.1 collective-permute-start.2
  27.3 2.6 %collective-permute-start.3 = (f32[16,3,1,4,128]{4,3,2,1,0:T(4,128)S(1)}, f32[16,3,1,4,128]{4,3,2,1,0:T(4,128)S(1)}, u32[]{:S(2)}, u32[]{:S(2)}) collective-permute-start(f32[16,3,1,4,128]{4,3,2,1,0:T(4,128)S(1)} %get-tuple-element.7), channel_id=1, source_target_pairs={{1,0},{2,1},{3,2},{4,3},{5,4},{6,5},{7,6},{0,7},{9,8},{10,9},{11,1... | collective-permute-start | bytes 294920 | tf_op jit(solution)/shard_map/ppermute | solution.py:22
  29.9 0.0 copy-done.1
  29.9 2.3 %collective-permute-done.2 = f32[16,3,1,4,128]{4,3,2,1,0:T(4,128)S(1)} collective-permute-done((f32[16,3,1,4,128]{4,3,2,1,0:T(4,128)S(1)}, f32[16,3,1,4,128]{4,3,2,1,0:T(4,128)S(1)}, u32[]{:S(2)}, u32[]{:S(2)}) %collective-permute-start.2) | collective-permute-done | bytes 98336 | tf_op jit(solution)/shard_map/ppermute | solution.py:19
  32.2 0.0 collective-permute-done.3
  32.2 2.1 %fusion.4 = f32[16,3,1,64,128]{4,3,2,1,0:T(8,128)S(1)} fusion(f32[16,3,1,64,128]{4,3,2,1,0:T(8,128)S(1)} %fusion.24, f32[16,3,1,4,128]{4,3,2,1,0:T(4,128)S(1)} %collective-permute-done.3, f32[16,3,1,4,128]{4,3,2,1,0:T(4,128)S(1)} %collective-permute-done.2, f32[128]{0:T(128)S(1)} %sqrt.3), kind=kLoop, calls=%fused_computation.29 | loop fusion | flops 10223616 | bytes 3342848 | tf_op jit(solution)/shard_map/mul | solution.py:43
  34.3 2.7 %fusion.52 = f32[16,16]{0,1:T(8,128)S(1)} fusion(f32[16,3,64,128]{3,2,1,0:T(8,128)S(1)} %bitcast.28), kind=kOutput, calls=%fused_computation.79 | convolution fusion | flops 75497472 | bytes 1573888 | tf_op jit(solution)/shard_map/dot_general | solution.py:45
  37.0 40.6 %psum.7 = f32[16,16]{0,1:T(8,128)S(1)} all-reduce(f32[16,16]{0,1:T(8,128)S(1)} %fusion.52), channel_id=1, replica_groups=mesh['gy'=4,'gz'=8] {'gy','gz'}, use_global_device_ids=true, to_apply=%region_0.0 | all-reduce | flops 256 | bytes 2048 | tf_op jit(solution)/shard_map/psum | solution.py:48
  77.6 0.1 copy.17
  77.7 1.5 %cholesky.16 = f32[16,16]{1,0:T(8,128)S(1)} custom-call(f32[16,16]{1,0:T(8,128)S(1)} %fusion.56), custom_call_target="Cholesky" | custom-call | tf_op jit(solution)/shard_map/jit(cholesky)/cholesky | solution.py:49
  79.2 0.6 compare_reduce_fusion
  79.8 0.7 multiply_bitcast_fusion
  80.5 1.2 %custom-call.6 = f32[1,16,16]{1,2,0:T(8,128)S(1)} custom-call(f32[1,16,16]{2,1,0:T(8,128)S(1)} %get-tuple-element.11), custom_call_target="InvertDiagBlocksLowerTriangular" | custom-call | tf_op jit(solution)/shard_map/triangular_solve | solution.py:51
  81.7 2.2 %fusion.49 = f32[2,8,192,128]{3,1,2,0:T(8,128)S(1)} fusion(f32[2,8,192,128]{3,2,1,0:T(8,128)S(1)} %bitcast.29, f32[1,16,16]{1,2,0:T(8,128)S(1)} %custom-call.6), kind=kOutput, calls=%fused_computation.78 | convolution fusion | flops 75890688 | bytes 3146752 | tf_op jit(solution)/shard_map/triangular_solve | solution.py:51
  83.9 1.4 %copy.25 = f32[2,8,192,128]{3,2,1,0:T(8,128)} copy(f32[2,8,192,128]{3,1,2,0:T(8,128)S(1)} %fusion.49) | data formatting | bytes 3145728
  85.4 0.7 copy.19
  (4 shorter events, 0.1 us)
Async XLA Ops:
  3.7 7.1 %collective-permute-start = (f32[16,3,1,64,4]{3,0,4,2,1:T(8,128)S(1)}, f32[16,3,1,64,4]{3,0,4,2,1:T(8,128)S(1)}, u32[]{:S(2)}, u32[]{:S(2)}) collective-permute-start(f32[16,3,1,64,4]{3,0,4,2,1:T(8,128)S(1)} %copy.22), channel_id=1, source_target_pairs={{0,8},{8,16},{16,24},{1,9},{9,17},{17,25},{2,10},{10,18},{18,26},{... | collective-permute-start | bytes 147464 | tf_op jit(solution)/shard_map/ppermute | solution.py:19
  9.1 8.3 %copy-start = (f32[16,3,1,64,128]{4,3,2,1,0:T(8,128)S(1)}, f32[16,3,1,64,128]{4,3,2,1,0:T(8,128)}, u32[]{:S(2)}) copy-start(f32[16,3,1,64,128]{4,3,2,1,0:T(8,128)} %param.2) | copy-start | bytes 4718596
  9.2 6.6 %collective-permute-start.1 = (f32[16,3,1,64,4]{3,0,4,2,1:T(8,128)S(1)}, f32[16,3,1,64,4]{3,0,4,2,1:T(8,128)S(1)}, u32[]{:S(2)}, u32[]{:S(2)}) collective-permute-start(f32[16,3,1,64,4]{3,0,4,2,1:T(8,128)S(1)} %copy.23), channel_id=1, source_target_pairs={{8,0},{16,8},{24,16},{9,1},{17,9},{25,17},{10,2},{18,10},{26,18},{... | collective-permute-start | bytes 147464 | tf_op jit(solution)/shard_map/ppermute | solution.py:22
  17.5 12.4 %copy-start.1 = (f32[128]{0:T(128)S(1)}, f32[128]{0:T(128)}, u32[]{:S(2)}) copy-start(f32[128]{0:T(128)} %param.3) | copy-start | bytes 1540
  27.2 5.0 %collective-permute-start.2 = (f32[16,3,1,4,128]{4,3,2,1,0:T(4,128)S(1)}, f32[16,3,1,4,128]{4,3,2,1,0:T(4,128)S(1)}, u32[]{:S(2)}, u32[]{:S(2)}) collective-permute-start(f32[16,3,1,4,128]{4,3,2,1,0:T(4,128)S(1)} %get-tuple-element.6), channel_id=1, source_target_pairs={{0,1},{1,2},{2,3},{3,4},{4,5},{5,6},{6,7},{7,0},{8,9},{9,10},{10,1... | collective-permute-start | bytes 294920 | tf_op jit(solution)/shard_map/ppermute | solution.py:19
  27.3 4.9 %collective-permute-start.3 = (f32[16,3,1,4,128]{4,3,2,1,0:T(4,128)S(1)}, f32[16,3,1,4,128]{4,3,2,1,0:T(4,128)S(1)}, u32[]{:S(2)}, u32[]{:S(2)}) collective-permute-start(f32[16,3,1,4,128]{4,3,2,1,0:T(4,128)S(1)} %get-tuple-element.7), channel_id=1, source_target_pairs={{1,0},{2,1},{3,2},{4,3},{5,4},{6,5},{7,6},{0,7},{9,8},{10,9},{11,1... | collective-permute-start | bytes 294920 | tf_op jit(solution)/shard_map/ppermute | solution.py:22
where the time goes:
time: 86.4 us; the launch traced here: 86 us
  blocking collectives  40.6 us (47%)
  other arithmetic  15.8 us (18%)
  starting transfers between devices  9.05 us (10%)
  local copies, waits for them, and re-layouts  8.04 us (9%)
  waiting for transfers between devices  6.95 us (8%)
  matrix products  4.91 us (6%)
    psum x1, blocking collectives, per_device(): summed_gram = lax.psum(gram_local, ('gy', 'gz'))  40.6 us
    add x1, other arithmetic, filter_axis(): sum((FILTER_TAPS[offset] * lax.slice_in_dim(padded, offset, offset + leng...  9.66 us
    ppermute x2, starting transfers between devices, with_halo(): lax.ppermute(lax.slice_in_dim(block, block.shape[dim] - width, None, axis...  4.99 us
    ppermute x2, waiting for transfers between devices, with_halo(): lax.ppermute(lax.slice_in_dim(block, 0, width, axis=dim), axis, backward)  4.43 us
    ppermute x2, starting transfers between devices, with_halo(): lax.ppermute(lax.slice_in_dim(block, 0, width, axis=dim), axis, backward)  4.06 us
    unnamed x8, local copies, waits for them, and re-layouts  3.17 us
    dot_general x1, matrix products, per_device(): jnp.dot(flat_rows, flat_rows.T, precision=lax.Precision.HIGHEST, preferre...  2.72 us
    slice x2, local copies, waits for them, and re-layouts, with_halo(): lax.slice_in_dim(block, block.shape[dim] - width, None, axis=dim)  2.55 us
  transfers between devices with their start and end apart: 4, of which 3 were waited for; matrix products, arithmetic and copies ran while one was open for 1% of the time, Pallas kernels for 0%

commit v1 on v0

v1 whole, which is shorter than its diff:
```python
import functools
import math

import jax
import jax.numpy as jnp
from jax import lax
from jax.experimental import pallas as pl
from jax.experimental.pallas import tpu as pltpu
from jax.sharding import PartitionSpec as P

FILTER_RAW = [math.exp(-(offset - 4) * (offset - 4) / 4.5) for offset in range(9)]
FILTER_TAPS = [value / sum(FILTER_RAW) for value in FILTER_RAW]
HALF_TAPS = FILTER_TAPS[4:]

MESH = pl.DeviceIdType.MESH
F32, BF16 = jnp.float32, jnp.bfloat16


def split(value):
    high = value.astype(BF16)
    return high, (value - high.astype(F32)).astype(BF16)


def band(distance):
    out = jnp.zeros(distance.shape, F32)
    for k in range(5):
        out = jnp.where(distance == k, HALF_TAPS[k], out)
    return out


def lane_roll(value, shift):
    flat = value.reshape(-1, value.shape[-1])
    return pltpu.roll(flat, shift, 1).reshape(value.shape)


def filter_z(ref, index, cells):
    out = HALF_TAPS[0] * ref[index, pl.ds(8, cells), :]
    for k in range(1, 5):
        out = out + HALF_TAPS[k] * (
            ref[index, pl.ds(8 - k, cells), :] + ref[index, pl.ds(8 + k, cells), :]
        )
    return out


def kernel(
    snaps, comps, row_total, x_ref, w_ref, modes_ref, factor_ref,
    field, pack_low, pack_high, side, corner, halo, rows, gram_z, gram_y,
    load_sem, halo_send, halo_recv, gz_send, gz_recv, gy_send, gy_recv,
):
    cells, width = x_ref.shape[1], x_ref.shape[2]
    half = cells // 2
    gy, gz = lax.axis_index("gy"), lax.axis_index("gz")
    ny, nz = lax.axis_size("gy"), lax.axis_size("gz")

    def gz_at(step):
        return lax.rem(gz + step + nz, nz)

    loads = []
    part = snaps * comps // 4
    for q in range(4):
        loads.append(pltpu.make_async_copy(
            x_ref.at[pl.ds(q * part, part)],
            field.at[pl.ds(q * part, part), pl.ds(8, cells)],
            load_sem.at[q],
        ))
        loads[-1].start()
    side[...] = jnp.zeros_like(side)
    corner[...] = jnp.zeros_like(corner)

    barrier = pltpu.get_barrier_semaphore()
    peers = [(gy, gz_at(d)) for d in range(1, nz)]
    peers += [(lax.rem(gy + d, ny), gz) for d in range(1, ny)]
    for d in (1, -1):
        peers += [(lax.rem(gy + d + ny, ny), gz_at(1)), (lax.rem(gy + d + ny, ny), gz_at(-1))]
    for peer in peers:
        pl.semaphore_signal(barrier, inc=1, device_id=peer, device_id_type=MESH)

    lane = lax.broadcasted_iota(jnp.int32, (1, width), 1)
    packed = jnp.zeros((comps * cells, width), F32)
    for s in range(snaps):
        if s % 4 == 0:
            loads[s // 4].wait()
        block = field[pl.ds(comps * s, comps), pl.ds(8, cells), :].reshape(comps * cells, width)
        packed = jnp.where(lane // 8 == s, pltpu.roll(block, (4 + 8 * s) % width, 1), packed)
    packed = packed.reshape(comps, cells, width)
    first, second = packed[:, :half], packed[:, half:]
    left_lanes = (lane % 8 < 4).reshape(1, 1, width)
    pack_high[...] = jnp.where(left_lanes, first, lane_roll(second, 4))
    pack_low[...] = jnp.where(left_lanes, lane_roll(second, width - 4), first)

    pl.semaphore_wait(barrier, len(peers))

    def remote(src, dst, n, target):
        return pltpu.make_async_remote_copy(
            src_ref=src, dst_ref=dst, send_sem=halo_send.at[n], recv_sem=halo_recv.at[n],
            device_id=target, device_id_type=MESH,
        )

    copies = [
        remote(x_ref.at[:, pl.ds(cells - 4, 4), :], field.at[:, pl.ds(4, 4), :], 0, (gy, gz_at(1))),
        remote(x_ref.at[:, pl.ds(0, 4), :], field.at[:, pl.ds(cells + 8, 4), :], 1, (gy, gz_at(-1))),
    ]
    up = jnp.minimum(gy + 1, ny - 1)
    down = jnp.maximum(gy - 1, 0)
    to_up = [
        remote(pack_high, side.at[0], 2, (up, gz)),
        remote(pack_high.at[:, pl.ds(half - 8, 8)], corner.at[0, 0], 3, (up, gz_at(1))),
        remote(pack_high.at[:, pl.ds(0, 8)], corner.at[0, 1], 4, (up, gz_at(-1))),
    ]
    to_down = [
        remote(pack_low, side.at[1], 5, (down, gz)),
        remote(pack_low.at[:, pl.ds(half - 8, 8)], corner.at[1, 0], 6, (down, gz_at(1))),
        remote(pack_low.at[:, pl.ds(0, 8)], corner.at[1, 1], 7, (down, gz_at(-1))),
    ]

    @pl.when(gy < ny - 1)
    def _():
        for copy in to_up:
            copy.start()

    @pl.when(gy > 0)
    def _():
        for copy in to_down:
            copy.start()

    for copy in copies:
        copy.start()

    root = jnp.sqrt(w_ref[...])
    row_i = lax.broadcasted_iota(jnp.int32, (width, width), 0)
    col_i = lax.broadcasted_iota(jnp.int32, (width, width), 1)
    j = row_i % 8
    position = jnp.where(j < 4, j - 4, width + j - 4)
    matrix = jnp.concatenate(
        [band(jnp.abs(row_i - col_i)) * root, band(jnp.abs(position - col_i)) * root], axis=0
    )
    matrix_high, matrix_low = split(matrix)
    matrix_both = jnp.concatenate([matrix_high, matrix_low], axis=1)

    @pl.when(gy > 0)
    def _():
        for copy in to_up:
            copy.wait_recv()

    @pl.when(gy < ny - 1)
    def _():
        for copy in to_down:
            copy.wait_recv()

    halo[:, pl.ds(0, 8), :] = jnp.where(
        left_lanes, lane_roll(corner[0, 0], width - 4), lane_roll(corner[1, 0], 4))
    halo[:, pl.ds(8, half), :] = jnp.where(left_lanes, side[0], side[1])
    halo[:, pl.ds(8 + half, half), :] = jnp.where(
        left_lanes, lane_roll(side[0], width - 4), lane_roll(side[1], 4))
    halo[:, pl.ds(8 + cells, 8), :] = jnp.where(left_lanes, corner[0, 1], corner[1, 1])
    halo_z = jnp.concatenate([filter_z(halo, c, cells) for c in range(comps)], axis=0)
    halo_high, halo_low = split(halo_z)

    for copy in copies:
        copy.wait_recv()

    def smooth_one(s, carry):
        field_z = jnp.concatenate(
            [filter_z(field, comps * s + c, cells) for c in range(comps)], axis=0)
        high, low = split(field_z)
        keep = (lane // 8 == s).astype(F32).astype(BF16)
        left = jnp.dot(
            jnp.concatenate([high, halo_high * keep], axis=1), matrix_both,
            preferred_element_type=F32)
        right = jnp.dot(
            jnp.concatenate([low, halo_low * keep], axis=1), matrix_high,
            preferred_element_type=F32)
        high, low = split(left[:, :width] + left[:, width:] + right)
        for n in range(comps * cells // 16):
            rows[s, :, pl.ds(2 * width * n, width)] = high[16 * n:16 * n + 16]
            rows[s, :, pl.ds(2 * width * n + width, width)] = low[16 * n:16 * n + 16]
        return carry

    lax.fori_loop(0, snaps, smooth_one, 0)

    chunks = comps * cells // 16
    size = snaps * 16
    both = rows[...].reshape(size, 2 * width * chunks)
    swapped = jnp.concatenate(
        [both[:, width * (n ^ 1):width * (n ^ 1) + width] for n in range(2 * chunks)], axis=1)
    dims = (((1,), (1,)), ((), ()))
    big = lax.dot_general(both, both, dims, preferred_element_type=F32)
    big = big + lax.dot_general(swapped, both, dims, preferred_element_type=F32)
    big_i = lax.broadcasted_iota(jnp.int32, (size, size), 0)
    big_j = lax.broadcasted_iota(jnp.int32, (size, size), 1)
    same = big_i % 16 == big_j % 16
    big = jnp.where(same, big, 0.0).reshape(snaps, 16, size).sum(axis=1)
    gather_i = lax.broadcasted_iota(jnp.int32, (size, width), 0)
    gather_j = lax.broadcasted_iota(jnp.int32, (size, width), 1)
    gather = (gather_i // 16 == gather_j).astype(F32)
    gram = jnp.dot(big, gather, precision=lax.Precision.HIGHEST, preferred_element_type=F32)

    def all_sum(value, slots, mine, count, send, recv, device):
        slots[mine] = value
        sent = []
        for d in range(1, count):
            copy = pltpu.make_async_remote_copy(
                src_ref=slots.at[mine], dst_ref=slots.at[mine],
                send_sem=send.at[d], recv_sem=recv.at[d],
                device_id=device(lax.rem(mine + d, count)), device_id_type=MESH,
            )
            copy.start()
            sent.append(copy)
        for copy in sent:
            copy.wait_recv()
        total = slots[0]
        for n in range(1, count):
            total = total + slots[n]
        return total, sent

    gram, sent_z = all_sum(gram, gram_z, gz, nz, gz_send, gz_recv, lambda n: (gy, n))
    gram, sent_y = all_sum(gram, gram_y, gy, ny, gy_send, gy_recv, lambda n: (n, gz))

    m_i = lax.broadcasted_iota(jnp.int32, (snaps, width), 0)
    m_j = lax.broadcasted_iota(jnp.int32, (snaps, width), 1)
    work = jnp.where(m_j == m_i + snaps, 1.0, gram)
    for k in range(snaps - 1):
        scaled = work[k:k + 1, :] / work[k:k + 1, k:k + 1]
        work = work - jnp.where(m_i > k, work[:, k:k + 1], 0.0) * scaled
    pivots = jnp.sum(jnp.where(m_i == m_j, work, 0.0), axis=1, keepdims=True)
    work = work / jnp.sqrt(pivots)
    upper = jnp.where(m_j >= m_i, work, 0.0) * (1.0 / math.sqrt(row_total))
    factor_ref[...] = upper[:, :snaps]

    inverse_high, inverse_low = split(work * math.sqrt(row_total))
    spread_i = lax.broadcasted_iota(jnp.int32, (width, size), 0)
    spread_j = lax.broadcasted_iota(jnp.int32, (width, size), 1)
    spread = (spread_i - snaps == spread_j // 16).astype(F32).astype(BF16)

    def blocks(value):
        tall = jnp.broadcast_to(
            value.astype(F32)[:, None, :], (snaps, 16, width)).reshape(size, width).astype(BF16)
        wide = jnp.dot(tall, spread, preferred_element_type=F32)
        return jnp.where(same, wide, 0.0).astype(BF16)

    inverse_high, inverse_low = blocks(inverse_high), blocks(inverse_low)
    for n in range(chunks):
        block = rows[:, :, pl.ds(2 * width * n, 2 * width)].reshape(size, 2 * width)
        left = jnp.dot(inverse_high, block, preferred_element_type=F32)
        right = jnp.dot(inverse_low, block[:, :width], preferred_element_type=F32)
        out = left[:, :width] + left[:, width:] + right
        modes_ref[:, pl.ds(16 * n, 16), :] = out.reshape(snaps, 16, width)

    for copy in copies + sent_z + sent_y:
        copy.wait_send()

    @pl.when(gy < ny - 1)
    def _():
        for copy in to_up:
            copy.wait_send()

    @pl.when(gy > 0)
    def _():
        for copy in to_down:
            copy.wait_send()


def per_device(snapshots, cell_weight):
    snaps, comps, planes, cells, width = snapshots.shape
    comps_all = comps * planes
    ny, nz = lax.axis_size("gy"), lax.axis_size("gz")
    row_total = comps_all * cells * width * ny * nz
    modes, factor = pl.pallas_call(
        functools.partial(kernel, snaps, comps_all, row_total),
        out_shape=(
            jax.ShapeDtypeStruct((snaps, comps_all * cells, width), F32),
            jax.ShapeDtypeStruct((snaps, snaps), F32),
        ),
        in_specs=[pl.BlockSpec(memory_space=pl.ANY), pl.BlockSpec(memory_space=pltpu.VMEM)],
        out_specs=(
            pl.BlockSpec(memory_space=pltpu.VMEM),
            pl.BlockSpec(memory_space=pltpu.VMEM),
        ),
        scratch_shapes=[
            pltpu.VMEM((snaps * comps_all, cells + 16, width), F32),
            pltpu.VMEM((comps_all, cells // 2, width), F32),
            pltpu.VMEM((comps_all, cells // 2, width), F32),
            pltpu.VMEM((2, comps_all, cells // 2, width), F32),
            pltpu.VMEM((2, 2, comps_all, 8, width), F32),
            pltpu.VMEM((comps_all, cells + 16, width), F32),
            pltpu.VMEM((snaps, 16, 2 * width * comps_all * cells // 16), BF16),
            pltpu.VMEM((nz, snaps, width), F32),
            pltpu.VMEM((ny, snaps, width), F32),
            pltpu.SemaphoreType.DMA((4,)),
            pltpu.SemaphoreType.DMA((8,)),
            pltpu.SemaphoreType.DMA((8,)),
            pltpu.SemaphoreType.DMA((nz,)),
            pltpu.SemaphoreType.DMA((nz,)),
            pltpu.SemaphoreType.DMA((ny,)),
            pltpu.SemaphoreType.DMA((ny,)),
        ],
        compiler_params=pltpu.CompilerParams(
            collective_id=0, has_side_effects=True, vmem_limit_bytes=40 * 1024 * 1024
        ),
    )(snapshots.reshape(snaps * comps_all, cells, width), cell_weight.reshape(1, width))
    return modes.reshape(snapshots.shape), factor


def solution(mesh):
    return jax.shard_map(
        per_device,
        mesh=mesh,
        in_specs=(P(None, None, None, "gz", "gy"), P("gy")),
        out_specs=(P(None, None, None, "gz", "gy"), P()),
        check_vma=False,
    )
```

time: 86.4 us -> 30.4 us (0.35)
  blocking collectives: 40.6 us -> 0 us
  Pallas kernels: 0 us -> 25.8 us
  other arithmetic: 15.8 us -> 0 us
  starting transfers between devices: 9.05 us -> 0 us
  waiting for transfers between devices: 6.95 us -> 0 us
  matrix products: 4.91 us -> 0 us
  local copies, waits for them, and re-layouts: 8.04 us -> 3.8 us
    psum x1 -> x0, blocking collectives: 40.6 us -> none  [per_device(): summed_gram = lax.psum(gram_local, ('gy', 'gz'))]
    pallas_call x0 -> x1, Pallas kernels: none -> 25.8 us  [per_device(): pl.pallas_call(functools.partial(kernel, snaps, comps_all, row_total), ou...]
    add x1 -> x0, other arithmetic: 9.66 us -> none  [filter_axis(): sum((FILTER_TAPS[offset] * lax.slice_in_dim(padded, offset, offset + leng...]
    ppermute x4 -> x0, starting transfers between devices: 9.05 us -> none  [the longest x2 4.99 us: with_halo(): lax.ppermute(lax.slice_in_dim(block, block.shape[dim] - width, None, axis...]
    ppermute x4 -> x0, waiting for transfers between devices: 6.95 us -> none  [the longest x2 4.43 us: with_halo(): lax.ppermute(lax.slice_in_dim(block, 0, width, axis=dim), axis, backward)]
    another operation x4 -> x0, other arithmetic: 3.36 us -> none  [the longest x3 2.13 us: per_device(): upper_factor = jnp.linalg.cholesky(summed_gram).T]
    dot_general x1 -> x0, matrix products: 2.72 us -> none  [per_device(): jnp.dot(flat_rows, flat_rows.T, precision=lax.Precision.HIGHEST, preferre...]
    slice x2 -> x0, local copies, waits for them, and re-layouts: 2.55 us -> none  [with_halo(): lax.slice_in_dim(block, block.shape[dim] - width, None, axis=dim)]
  transfers between devices with their start and end apart: 4 -> 0, of which waited for: 3 -> 0; matrix products, arithmetic and copies ran while one was open for 1% -> 0% of each run, Pallas kernels for 0% -> 0%
where the time goes in v1:
time: 30.4 us; the launch traced here: 30.2 us
  Pallas kernels  25.8 us (85%)
  local copies, waits for them, and re-layouts  3.8 us (12%)
  between operations  0.65 us (2%)
    pallas_call x1, Pallas kernels, per_device(): pl.pallas_call(functools.partial(kernel, snaps, comps_all, row_total), ou...  25.8 us
    unnamed x6, local copies, waits for them, and re-layouts  3.8 us

profile of v1, /device:TPU:0, one launch (start us, length us, event | category | flops | bytes accessed | tf_op | source)
XLA Modules:
  0.0 30.2 jit_solution(1899572597652040840)
XLA Ops:
  0.6 0.0 copy-start
  0.6 1.4 %copy-done = f32[16,3,1,64,128]{4,3,2,1,0:T(8,128)S(1)} copy-done((f32[16,3,1,64,128]{4,3,2,1,0:T(8,128)S(1)}, f32[16,3,1,64,128]{4,3,2,1,0:T(8,128)}, u32[]{:S(2)}) %copy-start) | copy-done | bytes 1572888
  2.0 0.0 copy-start.1
  2.0 0.7 %copy-done.1 = f32[128]{0:T(128)S(1)} copy-done((f32[128]{0:T(128)S(1)}, f32[128]{0:T(128)}, u32[]{:S(2)}) %copy-start.1) | copy-done | bytes 536
  2.7 25.8 %shard_map.41 = (f32[16,192,128]{2,1,0:T(8,128)S(1)}, f32[16,16]{1,0:T(8,128)S(1)}) custom-call(f32[48,64,128]{2,1,0:T(8,128)S(1)} %bitcast.5, f32[1,128]{1,0:T(1,128)S(1)} %bitcast.7), custom_call_target="tpu_custom_call" | custom-call | tf_op jit(solution)/shard_map/pallas_call | solution.py:268
  28.5 1.1 %copy.7 = f32[16,3,1,64,128]{4,3,2,1,0:T(8,128)} copy(f32[16,3,1,64,128]{4,3,2,1,0:T(8,128)S(1)} %bitcast.6) | data formatting | bytes 3145728
  29.6 0.6 %copy.8 = f32[16,16]{1,0:T(8,128)} copy(f32[16,16]{1,0:T(8,128)S(1)} %get-tuple-element.11) | data formatting | bytes 2048
Async XLA Ops:
  0.6 1.4 %copy-start = (f32[16,3,1,64,128]{4,3,2,1,0:T(8,128)S(1)}, f32[16,3,1,64,128]{4,3,2,1,0:T(8,128)}, u32[]{:S(2)}) copy-start(f32[16,3,1,64,128]{4,3,2,1,0:T(8,128)} %param.2) | copy-start | bytes 4718596
  2.0 0.7 %copy-start.1 = (f32[128]{0:T(128)S(1)}, f32[128]{0:T(128)}, u32[]{:S(2)}) copy-start(f32[128]{0:T(128)} %param.3) | copy-start | bytes 1540

commit v2 on v1

--- a/solution.py
+++ b/solution.py
@@ -42,10 +42,10 @@
     return out
 
 
-def kernel(
-    snaps, comps, row_total, x_ref, w_ref, modes_ref, factor_ref,
-    field, pack_low, pack_high, side, corner, halo, rows, gram_z, gram_y,
-    load_sem, halo_send, halo_recv, gz_send, gz_recv, gy_send, gy_recv,
+def rows_kernel(
+    snaps, comps, x_ref, w_ref, rows_high, rows_low, gram_ref,
+    field, weight, pack_low, pack_high, side, corner, halo, square, slots,
+    load_sem, halo_send, halo_recv, gram_send, gram_recv,
 ):
     cells, width = x_ref.shape[1], x_ref.shape[2]
     half = cells // 2
@@ -64,16 +64,24 @@
             load_sem.at[q],
         ))
         loads[-1].start()
+    load_weight = pltpu.make_async_copy(w_ref, weight, load_sem.at[4])
+    load_weight.start()
     side[...] = jnp.zeros_like(side)
     corner[...] = jnp.zeros_like(corner)
 
     barrier = pltpu.get_barrier_semaphore()
-    peers = [(gy, gz_at(d)) for d in range(1, nz)]
-    peers += [(lax.rem(gy + d, ny), gz) for d in range(1, ny)]
-    for d in (1, -1):
-        peers += [(lax.rem(gy + d + ny, ny), gz_at(1)), (lax.rem(gy + d + ny, ny), gz_at(-1))]
-    for peer in peers:
-        pl.semaphore_signal(barrier, inc=1, device_id=peer, device_id_type=MESH)
+    devices = ny * nz
+    mine = gy * nz + gz
+
+    def device_at(step):
+        flat = lax.rem(mine + step, devices)
+        return flat // nz, lax.rem(flat, nz)
+
+    def greet(step, carry):
+        pl.semaphore_signal(barrier, inc=1, device_id=device_at(step), device_id_type=MESH)
+        return carry
+
+    lax.fori_loop(1, devices, greet, 0, unroll=devices <= 64)
 
     lane = lax.broadcasted_iota(jnp.int32, (1, width), 1)
     packed = jnp.zeros((comps * cells, width), F32)
@@ -88,7 +96,7 @@
     pack_high[...] = jnp.where(left_lanes, first, lane_roll(second, 4))
     pack_low[...] = jnp.where(left_lanes, lane_roll(second, width - 4), first)
 
-    pl.semaphore_wait(barrier, len(peers))
+    pl.semaphore_wait(barrier, devices - 1)
 
     def remote(src, dst, n, target):
         return pltpu.make_async_remote_copy(
@@ -126,7 +134,8 @@
     for copy in copies:
         copy.start()
 
-    root = jnp.sqrt(w_ref[...])
+    load_weight.wait()
+    root = jnp.sqrt(weight[...])
     row_i = lax.broadcasted_iota(jnp.int32, (width, width), 0)
     col_i = lax.broadcasted_iota(jnp.int32, (width, width), 1)
     j = row_i % 8
@@ -170,54 +179,101 @@
         right = jnp.dot(
             jnp.concatenate([low, halo_low * keep], axis=1), matrix_high,
             preferred_element_type=F32)
-        high, low = split(left[:, :width] + left[:, width:] + right)
+        smooth = left[:, :width] + left[:, width:] + right
+        high = smooth.astype(BF16)
+        rest = smooth - high.astype(F32)
+        low = rest.astype(BF16)
+        square[s] = (rest * rest).reshape(-1, 8, width).sum(axis=0)
         for n in range(comps * cells // 16):
-            rows[s, :, pl.ds(2 * width * n, width)] = high[16 * n:16 * n + 16]
-            rows[s, :, pl.ds(2 * width * n + width, width)] = low[16 * n:16 * n + 16]
+            rows_high[s, :, pl.ds(width * n, width)] = high[16 * n:16 * n + 16]
+            rows_low[s, :, pl.ds(width * n, width)] = low[16 * n:16 * n + 16]
         return carry
 
     lax.fori_loop(0, snaps, smooth_one, 0)
 
     chunks = comps * cells // 16
     size = snaps * 16
-    both = rows[...].reshape(size, 2 * width * chunks)
-    swapped = jnp.concatenate(
-        [both[:, width * (n ^ 1):width * (n ^ 1) + width] for n in range(2 * chunks)], axis=1)
+    high = rows_high[...].reshape(size, width * chunks)
+    low = rows_low[...].reshape(size, width * chunks)
     dims = (((1,), (1,)), ((), ()))
-    big = lax.dot_general(both, both, dims, preferred_element_type=F32)
-    big = big + lax.dot_general(swapped, both, dims, preferred_element_type=F32)
     big_i = lax.broadcasted_iota(jnp.int32, (size, size), 0)
     big_j = lax.broadcasted_iota(jnp.int32, (size, size), 1)
     same = big_i % 16 == big_j % 16
-    big = jnp.where(same, big, 0.0).reshape(snaps, 16, size).sum(axis=1)
+
+    def equal_z(left, right):
+        big = lax.dot_general(left, right, dims, preferred_element_type=F32)
+        return jnp.where(same, big, 0.0).reshape(snaps, 16, size).sum(axis=1)
+
+    main, cross = equal_z(high, high), equal_z(low, high)
+    groups = width // snaps
     gather_i = lax.broadcasted_iota(jnp.int32, (size, width), 0)
     gather_j = lax.broadcasted_iota(jnp.int32, (size, width), 1)
-    gather = (gather_i // 16 == gather_j).astype(F32)
-    gram = jnp.dot(big, gather, precision=lax.Precision.HIGHEST, preferred_element_type=F32)
-
-    def all_sum(value, slots, mine, count, send, recv, device):
-        slots[mine] = value
-        sent = []
-        for d in range(1, count):
-            copy = pltpu.make_async_remote_copy(
-                src_ref=slots.at[mine], dst_ref=slots.at[mine],
-                send_sem=send.at[d], recv_sem=recv.at[d],
-                device_id=device(lax.rem(mine + d, count)), device_id_type=MESH,
-            )
-            copy.start()
-            sent.append(copy)
-        for copy in sent:
-            copy.wait_recv()
-        total = slots[0]
-        for n in range(1, count):
-            total = total + slots[n]
-        return total, sent
-
-    gram, sent_z = all_sum(gram, gram_z, gz, nz, gz_send, gz_recv, lambda n: (gy, n))
-    gram, sent_y = all_sum(gram, gram_y, gy, ny, gy_send, gy_recv, lambda n: (n, gz))
-
+    gather = (gather_i // 16 == gather_j % snaps).astype(F32)
+    other_i = lax.broadcasted_iota(jnp.int32, (snaps, size), 0)
+    other_j = lax.broadcasted_iota(jnp.int32, (snaps, size), 1)
+    other = (other_j // 16 == other_i).astype(F32)
+    gram = jnp.dot(
+        main + cross, gather, precision=lax.Precision.HIGHEST, preferred_element_type=F32)
+    gram = gram + lax.dot_general(
+        other, jnp.concatenate([cross] * groups, axis=0), dims,
+        precision=lax.Precision.HIGHEST, preferred_element_type=F32)
+    g_i = lax.broadcasted_iota(jnp.int32, (snaps, width), 0)
+    g_j = lax.broadcasted_iota(jnp.int32, (snaps, width), 1)
+    squares = jnp.sum(jnp.sum(square[...], axis=1), axis=1, keepdims=True)
+    gram = gram + jnp.where(g_j % snaps == g_i, squares, 0.0)
+    gram = jnp.where((g_j // snaps + g_i) % groups == 0, gram, 0.0)
+    slots[mine] = gram.reshape(snaps // groups, groups, width).sum(axis=1)
+
+    def share(step):
+        return pltpu.make_async_remote_copy(
+            src_ref=slots.at[mine], dst_ref=slots.at[mine],
+            send_sem=gram_send.at[step], recv_sem=gram_recv.at[step],
+            device_id=device_at(step), device_id_type=MESH,
+        )
+
+    def each(act):
+        def body(step, carry):
+            act(share(step))
+            return carry
+        lax.fori_loop(1, devices, body, 0, unroll=devices <= 64)
+
+    each(lambda copy: copy.start())
+    each(lambda copy: copy.wait_recv())
+    gram_ref[...] = jnp.sum(slots[...], axis=0)
+
+    each(lambda copy: copy.wait_send())
+    for copy in copies:
+        copy.wait_send()
+
+    @pl.when(gy < ny - 1)
+    def _():
+        for copy in to_up:
+            copy.wait_send()
+
+    @pl.when(gy > 0)
+    def _():
+        for copy in to_down:
+            copy.wait_send()
+
+
+def modes_kernel(
+    snaps, row_total, rows_high, rows_low, gram_ref, modes_ref, factor_ref,
+    modes, factor, out_sem,
+):
+    width = gram_ref.shape[1]
+    groups = width // snaps
+    size = snaps * 16
+    chunks = rows_high.shape[2] // width
     m_i = lax.broadcasted_iota(jnp.int32, (snaps, width), 0)
     m_j = lax.broadcasted_iota(jnp.int32, (snaps, width), 1)
+    gram = jnp.concatenate([
+        pltpu.roll(
+            jnp.broadcast_to(gram_ref[n:n + 1, :], (groups, width)), 0, 1,
+            stride=snaps, stride_axis=0)
+        for n in range(snaps // groups)
+    ], axis=0)
+    gram = jnp.where(m_j < snaps, gram, 0.0)
+
     work = jnp.where(m_j == m_i + snaps, 1.0, gram)
     for k in range(snaps - 1):
         scaled = work[k:k + 1, :] / work[k:k + 1, k:k + 1]
@@ -225,12 +281,18 @@
     pivots = jnp.sum(jnp.where(m_i == m_j, work, 0.0), axis=1, keepdims=True)
     work = work / jnp.sqrt(pivots)
     upper = jnp.where(m_j >= m_i, work, 0.0) * (1.0 / math.sqrt(row_total))
-    factor_ref[...] = upper[:, :snaps]
+    factor[...] = upper[:, :snaps]
+    copies = [pltpu.make_async_copy(factor, factor_ref, out_sem.at[0])]
+    copies[0].start()
 
     inverse_high, inverse_low = split(work * math.sqrt(row_total))
     spread_i = lax.broadcasted_iota(jnp.int32, (width, size), 0)
     spread_j = lax.broadcasted_iota(jnp.int32, (width, size), 1)
     spread = (spread_i - snaps == spread_j // 16).astype(F32).astype(BF16)
+
+    same_i = lax.broadcasted_iota(jnp.int32, (size, size), 0)
+    same_j = lax.broadcasted_iota(jnp.int32, (size, size), 1)
+    same = same_i % 16 == same_j % 16
 
     def blocks(value):
         tall = jnp.broadcast_to(
@@ -239,25 +301,24 @@
         return jnp.where(same, wide, 0.0).astype(BF16)
 
     inverse_high, inverse_low = blocks(inverse_high), blocks(inverse_low)
-    for n in range(chunks):
-        block = rows[:, :, pl.ds(2 * width * n, 2 * width)].reshape(size, 2 * width)
-        left = jnp.dot(inverse_high, block, preferred_element_type=F32)
-        right = jnp.dot(inverse_low, block[:, :width], preferred_element_type=F32)
-        out = left[:, :width] + left[:, width:] + right
-        modes_ref[:, pl.ds(16 * n, 16), :] = out.reshape(snaps, 16, width)
-
-    for copy in copies + sent_z + sent_y:
-        copy.wait_send()
-
-    @pl.when(gy < ny - 1)
-    def _():
-        for copy in to_up:
-            copy.wait_send()
-
-    @pl.when(gy > 0)
-    def _():
-        for copy in to_down:
-            copy.wait_send()
+    parts = out_sem.shape[0] - 1
+    for q in range(parts):
+        depth = chunks // parts
+        for n in range(q * depth, (q + 1) * depth, 2):
+            high = rows_high[:, :, pl.ds(width * n, 2 * width)].reshape(size, 2 * width)
+            low = rows_low[:, :, pl.ds(width * n, 2 * width)].reshape(size, 2 * width)
+            out = jnp.dot(inverse_high, high, preferred_element_type=F32)
+            out = out + jnp.dot(inverse_high, low, preferred_element_type=F32)
+            out = out + jnp.dot(inverse_low, high, preferred_element_type=F32)
+            for m in range(2):
+                modes[:, pl.ds(16 * (n + m), 16), :] = out[
+                    :, m * width:(m + 1) * width].reshape(snaps, 16, width)
+        span = pl.ds(16 * q * depth, 16 * depth)
+        copies.append(pltpu.make_async_copy(
+            modes.at[:, span], modes_ref.at[:, span], out_sem.at[q + 1]))
+        copies[-1].start()
+    for copy in copies:
+        copy.wait()
 
 
 def per_device(snapshots, cell_weight):
@@ -265,39 +326,54 @@
     comps_all = comps * planes
     ny, nz = lax.axis_size("gy"), lax.axis_size("gz")
     row_total = comps_all * cells * width * ny * nz
-    modes, factor = pl.pallas_call(
-        functools.partial(kernel, snaps, comps_all, row_total),
+    devices = ny * nz
+    depth = width * comps_all * cells // 16
+    vmem = pl.BlockSpec(memory_space=pltpu.VMEM)
+    hbm = pl.BlockSpec(memory_space=pltpu.HBM)
+    rows_high, rows_low, gram = pl.pallas_call(
+        functools.partial(rows_kernel, snaps, comps_all),
         out_shape=(
-            jax.ShapeDtypeStruct((snaps, comps_all * cells, width), F32),
-            jax.ShapeDtypeStruct((snaps, snaps), F32),
+            jax.ShapeDtypeStruct((snaps, 16, depth), BF16),
+            jax.ShapeDtypeStruct((snaps, 16, depth), BF16),
+            jax.ShapeDtypeStruct((snaps * snaps // width, width), F32),
         ),
-        in_specs=[pl.BlockSpec(memory_space=pl.ANY), pl.BlockSpec(memory_space=pltpu.VMEM)],
-        out_specs=(
-            pl.BlockSpec(memory_space=pltpu.VMEM),
-            pl.BlockSpec(memory_space=pltpu.VMEM),
-        ),
+        in_specs=[hbm, hbm],
+        out_specs=(vmem, vmem, vmem),
         scratch_shapes=[
             pltpu.VMEM((snaps * comps_all, cells + 16, width), F32),
+            pltpu.VMEM((1, width), F32),
             pltpu.VMEM((comps_all, cells // 2, width), F32),
             pltpu.VMEM((comps_all, cells // 2, width), F32),
             pltpu.VMEM((2, comps_all, cells // 2, width), F32),
             pltpu.VMEM((2, 2, comps_all, 8, width), F32),
             pltpu.VMEM((comps_all, cells + 16, width), F32),
-            pltpu.VMEM((snaps, 16, 2 * width * comps_all * cells // 16), BF16),
-            pltpu.VMEM((nz, snaps, width), F32),
-            pltpu.VMEM((ny, snaps, width), F32),
-            pltpu.SemaphoreType.DMA((4,)),
+            pltpu.VMEM((snaps, 8, width), F32),
+            pltpu.VMEM((devices, snaps * snaps // width, width), F32),
+            pltpu.SemaphoreType.DMA((5,)),
             pltpu.SemaphoreType.DMA((8,)),
             pltpu.SemaphoreType.DMA((8,)),
-            pltpu.SemaphoreType.DMA((nz,)),
-            pltpu.SemaphoreType.DMA((nz,)),
-            pltpu.SemaphoreType.DMA((ny,)),
-            pltpu.SemaphoreType.DMA((ny,)),
+            pltpu.SemaphoreType.DMA((devices,)),
+            pltpu.SemaphoreType.DMA((devices,)),
         ],
         compiler_params=pltpu.CompilerParams(
-            collective_id=0, has_side_effects=True, vmem_limit_bytes=40 * 1024 * 1024
+            collective_id=0, has_side_effects=True, vmem_limit_bytes=32 * 1024 * 1024
         ),
     )(snapshots.reshape(snaps * comps_all, cells, width), cell_weight.reshape(1, width))
+    modes, factor = pl.pallas_call(
+        functools.partial(modes_kernel, snaps, row_total),
+        out_shape=(
+            jax.ShapeDtypeStruct((snaps, comps_all * cells, width), F32),
+            jax.ShapeDtypeStruct((snaps, snaps), F32),
+        ),
+        in_specs=[vmem, vmem, vmem],
+        out_specs=(hbm, hbm),
+        scratch_shapes=[
+            pltpu.VMEM((snaps, comps_all * cells, width), F32),
+            pltpu.VMEM((snaps, snaps), F32),
+            pltpu.SemaphoreType.DMA((4,)),
+        ],
+        compiler_params=pltpu.CompilerParams(vmem_limit_bytes=32 * 1024 * 1024),
+    )(rows_high, rows_low, gram)
     return modes.reshape(snapshots.shape), factor
 
 

time: 30.4 us -> 26.1 us (0.86)
  Pallas kernels: 25.8 us -> 23.2 us
  local copies, waits for them, and re-layouts: 3.8 us -> 2.06 us
    pallas_call x1 -> x2, Pallas kernels: 25.8 us -> 23.2 us  [the longest x1 20.1 us: per_device(): pl.pallas_call(functools.partial(rows_kernel, snaps, comps_all), out_shap...]
    unnamed x6 -> x4, local copies, waits for them, and re-layouts: 3.8 us -> 2.06 us
where the time goes in v2:
time: 26.1 us; the launch traced here: 25.9 us
  Pallas kernels  23.2 us (89%)
  local copies, waits for them, and re-layouts  2.06 us (8%)
  between operations  0.65 us (2%)
    pallas_call x1, Pallas kernels, per_device(): pl.pallas_call(functools.partial(rows_kernel, snaps, comps_all), out_shap...  20.1 us
    pallas_call x1, Pallas kernels, per_device(): pl.pallas_call(functools.partial(modes_kernel, snaps, row_total), out_sha...  3.05 us
    unnamed x4, local copies, waits for them, and re-layouts  2.06 us

profile of v2, /device:TPU:0, one launch (start us, length us, event | category | flops | bytes accessed | tf_op | source)
XLA Modules:
  0.0 25.9 jit_solution(8029177706787402586)
XLA Ops:
  0.6 0.0 copy-start
  0.6 1.4 %copy-done = f32[16,3,1,64,128]{4,3,2,1,0:T(8,128)S(1)} copy-done((f32[16,3,1,64,128]{4,3,2,1,0:T(8,128)S(1)}, f32[16,3,1,64,128]{4,3,2,1,0:T(8,128)}, u32[]{:S(2)}) %copy-start) | copy-done | bytes 1572888
  2.0 0.0 copy-start.1
  2.0 0.7 %copy-done.1 = f32[128]{0:T(128)S(1)} copy-done((f32[128]{0:T(128)S(1)}, f32[128]{0:T(128)}, u32[]{:S(2)}) %copy-start.1) | copy-done | bytes 536
  2.7 20.1 %shard_map.41 = (bf16[16,16,1536]{2,1,0:T(8,128)(2,1)S(1)}, bf16[16,16,1536]{2,1,0:T(8,128)(2,1)S(1)}, f32[2,128]{1,0:T(2,128)S(1)}) custom-call(f32[48,64,128]{2,1,0:T(8,128)S(1)} %bitcast.5, f32[1,128]{1,0:T(1,128)S(1)} %bitcast.6), custom_call_target="tpu_custom_call" | custom-call | tf_op jit(solution)/shard_map/pallas_call | solution.py:333
  22.8 3.1 %shard_map.42 = (f32[16,192,128]{2,1,0:T(8,128)}, f32[16,16]{1,0:T(8,128)}) custom-call(bf16[16,16,1536]{2,1,0:T(8,128)(2,1)S(1)} %get-tuple-element.7.rows_high, bf16[16,16,1536]{2,1,0:T(8,128)(2,1)S(1)} %get-tuple-element.8.rows_low, f32[2,128]{1,0:T(2,128)S(1)} %get-tuple-element.9.gram_ref), custom_call_target="tpu_custom_call" | custom-call | tf_op jit(solution)/shard_map/pallas_call | solution.py:362
Async XLA Ops:
  0.6 1.4 %copy-start = (f32[16,3,1,64,128]{4,3,2,1,0:T(8,128)S(1)}, f32[16,3,1,64,128]{4,3,2,1,0:T(8,128)}, u32[]{:S(2)}) copy-start(f32[16,3,1,64,128]{4,3,2,1,0:T(8,128)} %param.2) | copy-start | bytes 4718596
  2.0 0.7 %copy-start.1 = (f32[128]{0:T(128)S(1)}, f32[128]{0:T(128)}, u32[]{:S(2)}) copy-start(f32[128]{0:T(128)} %param.3) | copy-start | bytes 1540

commit v3 on v2

--- a/solution.py
+++ b/solution.py
@@ -43,9 +43,9 @@
 
 
 def rows_kernel(
-    snaps, comps, x_ref, w_ref, rows_high, rows_low, gram_ref,
-    field, weight, pack_low, pack_high, side, corner, halo, square, slots,
-    load_sem, halo_send, halo_recv, gram_send, gram_recv,
+    snaps, comps, x_ref, w_ref, high_ref, low_ref, gram_ref,
+    field, rows_high, rows_low, weight, pack_low, pack_high, side, corner, halo, square, slots,
+    load_sem, store_sem, halo_send, halo_recv, gram_send, gram_recv,
 ):
     cells, width = x_ref.shape[1], x_ref.shape[2]
     half = cells // 2
@@ -191,6 +191,13 @@
 
     lax.fori_loop(0, snaps, smooth_one, 0)
 
+    stores = [
+        pltpu.make_async_copy(rows_high, high_ref, store_sem.at[0]),
+        pltpu.make_async_copy(rows_low, low_ref, store_sem.at[1]),
+    ]
+    for store in stores:
+        store.start()
+
     chunks = comps * cells // 16
     size = snaps * 16
     high = rows_high[...].reshape(size, width * chunks)
@@ -241,6 +248,8 @@
     each(lambda copy: copy.wait_recv())
     gram_ref[...] = jnp.sum(slots[...], axis=0)
 
+    for store in stores:
+        store.wait()
     each(lambda copy: copy.wait_send())
     for copy in copies:
         copy.wait_send()
@@ -257,9 +266,15 @@
 
 
 def modes_kernel(
-    snaps, row_total, rows_high, rows_low, gram_ref, modes_ref, factor_ref,
-    modes, factor, out_sem,
+    snaps, row_total, high_ref, low_ref, gram_ref, modes_ref, factor_ref,
+    rows_high, rows_low, modes, factor, load_sem, out_sem,
 ):
+    loads = [
+        pltpu.make_async_copy(high_ref, rows_high, load_sem.at[0]),
+        pltpu.make_async_copy(low_ref, rows_low, load_sem.at[1]),
+    ]
+    for load in loads:
+        load.start()
     width = gram_ref.shape[1]
     groups = width // snaps
     size = snaps * 16
@@ -301,6 +316,8 @@
         return jnp.where(same, wide, 0.0).astype(BF16)
 
     inverse_high, inverse_low = blocks(inverse_high), blocks(inverse_low)
+    for load in loads:
+        load.wait()
     parts = out_sem.shape[0] - 1
     for q in range(parts):
         depth = chunks // parts
@@ -338,9 +355,11 @@
             jax.ShapeDtypeStruct((snaps * snaps // width, width), F32),
         ),
         in_specs=[hbm, hbm],
-        out_specs=(vmem, vmem, vmem),
+        out_specs=(hbm, hbm, vmem),
         scratch_shapes=[
             pltpu.VMEM((snaps * comps_all, cells + 16, width), F32),
+            pltpu.VMEM((snaps, 16, depth), BF16),
+            pltpu.VMEM((snaps, 16, depth), BF16),
             pltpu.VMEM((1, width), F32),
             pltpu.VMEM((comps_all, cells // 2, width), F32),
             pltpu.VMEM((comps_all, cells // 2, width), F32),
@@ -350,13 +369,14 @@
             pltpu.VMEM((snaps, 8, width), F32),
             pltpu.VMEM((devices, snaps * snaps // width, width), F32),
             pltpu.SemaphoreType.DMA((5,)),
+            pltpu.SemaphoreType.DMA((2,)),
             pltpu.SemaphoreType.DMA((8,)),
             pltpu.SemaphoreType.DMA((8,)),
             pltpu.SemaphoreType.DMA((devices,)),
             pltpu.SemaphoreType.DMA((devices,)),
         ],
         compiler_params=pltpu.CompilerParams(
-            collective_id=0, has_side_effects=True, vmem_limit_bytes=32 * 1024 * 1024
+            collective_id=0, has_side_effects=True, vmem_limit_bytes=60 * 1024 * 1024
         ),
     )(snapshots.reshape(snaps * comps_all, cells, width), cell_weight.reshape(1, width))
     modes, factor = pl.pallas_call(
@@ -365,14 +385,17 @@
             jax.ShapeDtypeStruct((snaps, comps_all * cells, width), F32),
             jax.ShapeDtypeStruct((snaps, snaps), F32),
         ),
-        in_specs=[vmem, vmem, vmem],
+        in_specs=[hbm, hbm, vmem],
         out_specs=(hbm, hbm),
         scratch_shapes=[
+            pltpu.VMEM((snaps, 16, depth), BF16),
+            pltpu.VMEM((snaps, 16, depth), BF16),
             pltpu.VMEM((snaps, comps_all * cells, width), F32),
             pltpu.VMEM((snaps, snaps), F32),
+            pltpu.SemaphoreType.DMA((2,)),
             pltpu.SemaphoreType.DMA((4,)),
         ],
-        compiler_params=pltpu.CompilerParams(vmem_limit_bytes=32 * 1024 * 1024),
+        compiler_params=pltpu.CompilerParams(vmem_limit_bytes=60 * 1024 * 1024),
     )(rows_high, rows_low, gram)
     return modes.reshape(snapshots.shape), factor
 

time: 26.1 us -> 25.3 us (0.969)
  local copies, waits for them, and re-layouts: 2.06 us -> 0 us
  Pallas kernels: 23.2 us -> 24.5 us
    unnamed x4 -> x0, local copies, waits for them, and re-layouts: 2.06 us -> none
    pallas_call x1, Pallas kernels: 3.05 us -> 3.82 us  [per_device(): pl.pallas_call(functools.partial(modes_kernel, snaps, row_total), out_sha...]
    pallas_call x1, Pallas kernels: 20.1 us -> 20.7 us  [per_device(): pl.pallas_call(functools.partial(rows_kernel, snaps, comps_all), out_shap...]
where the time goes in v3:
time: 25.3 us; the launch traced here: 25.2 us
  Pallas kernels  24.5 us (97%)
  between operations  0.64 us (3%)
    pallas_call x1, Pallas kernels, per_device(): pl.pallas_call(functools.partial(rows_kernel, snaps, comps_all), out_shap...  20.7 us
    pallas_call x1, Pallas kernels, per_device(): pl.pallas_call(functools.partial(modes_kernel, snaps, row_total), out_sha...  3.82 us

profile of v3, /device:TPU:0, one launch (start us, length us, event | category | flops | bytes accessed | tf_op | source)
XLA Modules:
  0.0 25.2 jit_solution(10156156477226067351)
XLA Ops:
  0.6 20.7 %shard_map.41 = (bf16[16,16,1536]{2,1,0:T(8,128)(2,1)}, bf16[16,16,1536]{2,1,0:T(8,128)(2,1)}, f32[2,128]{1,0:T(2,128)}) custom-call(f32[48,64,128]{2,1,0:T(8,128)} %bitcast.5, f32[1,128]{1,0:T(1,128)} %bitcast.6), custom_call_target="tpu_custom_call" | custom-call | tf_op jit(solution)/shard_map/pallas_call | solution.py:350
  21.4 3.8 %shard_map.42 = (f32[16,192,128]{2,1,0:T(8,128)}, f32[16,16]{1,0:T(8,128)}) custom-call(bf16[16,16,1536]{2,1,0:T(8,128)(2,1)} %get-tuple-element.7.high_ref, bf16[16,16,1536]{2,1,0:T(8,128)(2,1)} %get-tuple-element.8.low_ref, f32[2,128]{1,0:T(2,128)} %get-tuple-element.9.gram_ref), custom_call_target="tpu_custom_call" | custom-call | tf_op jit(solution)/shard_map/pallas_call | solution.py:382

commit v4 on v3

--- a/solution.py
+++ b/solution.py
@@ -33,18 +33,24 @@
     return pltpu.roll(flat, shift, 1).reshape(value.shape)
 
 
-def filter_z(ref, index, cells):
-    out = HALF_TAPS[0] * ref[index, pl.ds(8, cells), :]
+def filter_z(ref, index, start, cells):
+    out = HALF_TAPS[0] * ref[index, pl.ds(8 + start, cells), :]
     for k in range(1, 5):
         out = out + HALF_TAPS[k] * (
-            ref[index, pl.ds(8 - k, cells), :] + ref[index, pl.ds(8 + k, cells), :]
+            ref[index, pl.ds(8 + start - k, cells), :] + ref[index, pl.ds(8 + start + k, cells), :]
         )
     return out
 
 
+def product(high, low, both, width):
+    out = jnp.dot(high, both, preferred_element_type=F32)
+    return out[:, :width] + out[:, width:] + jnp.dot(
+        low, both[:, :width], preferred_element_type=F32)
+
+
 def rows_kernel(
     snaps, comps, x_ref, w_ref, high_ref, low_ref, gram_ref,
-    field, rows_high, rows_low, weight, pack_low, pack_high, side, corner, halo, square, slots,
+    field, rows_high, rows_low, inner, weight, pack_low, pack_high, side, corner, halo, square, slots,
     load_sem, store_sem, halo_send, halo_recv, gram_send, gram_recv,
 ):
     cells, width = x_ref.shape[1], x_ref.shape[2]
@@ -140,11 +146,18 @@
     col_i = lax.broadcasted_iota(jnp.int32, (width, width), 1)
     j = row_i % 8
     position = jnp.where(j < 4, j - 4, width + j - 4)
-    matrix = jnp.concatenate(
-        [band(jnp.abs(row_i - col_i)) * root, band(jnp.abs(position - col_i)) * root], axis=0
-    )
-    matrix_high, matrix_low = split(matrix)
-    matrix_both = jnp.concatenate([matrix_high, matrix_low], axis=1)
+    own_both = jnp.concatenate(split(band(jnp.abs(row_i - col_i)) * root), axis=1)
+    halo_both = jnp.concatenate(split(band(jnp.abs(position - col_i)) * root), axis=1)
+
+    deep = cells - 16
+
+    def smooth_inner(s, carry):
+        high, low = split(jnp.concatenate(
+            [filter_z(field, comps * s + c, 8, deep) for c in range(comps)], axis=0))
+        inner[s] = product(high, low, own_both, width)
+        return carry
+
+    lax.fori_loop(0, snaps, smooth_inner, 0, unroll=True)
 
     @pl.when(gy > 0)
     def _():
@@ -162,24 +175,26 @@
     halo[:, pl.ds(8 + half, half), :] = jnp.where(
         left_lanes, lane_roll(side[0], width - 4), lane_roll(side[1], 4))
     halo[:, pl.ds(8 + cells, 8), :] = jnp.where(left_lanes, corner[0, 1], corner[1, 1])
-    halo_z = jnp.concatenate([filter_z(halo, c, cells) for c in range(comps)], axis=0)
+    halo_z = jnp.concatenate([filter_z(halo, c, 0, cells) for c in range(comps)], axis=0)
     halo_high, halo_low = split(halo_z)
 
     for copy in copies:
         copy.wait_recv()
 
     def smooth_one(s, carry):
-        field_z = jnp.concatenate(
-            [filter_z(field, comps * s + c, cells) for c in range(comps)], axis=0)
-        high, low = split(field_z)
+        high, low = split(jnp.concatenate(
+            [filter_z(field, comps * s + c, z, 8) for c in range(comps) for z in (0, cells - 8)],
+            axis=0))
+        edge = product(high, low, own_both, width)
         keep = (lane // 8 == s).astype(F32).astype(BF16)
-        left = jnp.dot(
-            jnp.concatenate([high, halo_high * keep], axis=1), matrix_both,
-            preferred_element_type=F32)
-        right = jnp.dot(
-            jnp.concatenate([low, halo_low * keep], axis=1), matrix_high,
-            preferred_element_type=F32)
-        smooth = left[:, :width] + left[:, width:] + right
+        smooth = product(halo_high * keep, halo_low * keep, halo_both, width)
+        own = []
+        for c in range(comps):
+            own += [
+                edge[16 * c:16 * c + 8], inner[s, pl.ds(deep * c, deep), :],
+                edge[16 * c + 8:16 * c + 16],
+            ]
+        smooth = smooth + jnp.concatenate(own, axis=0)
         high = smooth.astype(BF16)
         rest = smooth - high.astype(F32)
         low = rest.astype(BF16)
@@ -189,7 +204,7 @@
             rows_low[s, :, pl.ds(width * n, width)] = low[16 * n:16 * n + 16]
         return carry
 
-    lax.fori_loop(0, snaps, smooth_one, 0)
+    lax.fori_loop(0, snaps, smooth_one, 0, unroll=True)
 
     stores = [
         pltpu.make_async_copy(rows_high, high_ref, store_sem.at[0]),
@@ -360,6 +375,7 @@
             pltpu.VMEM((snaps * comps_all, cells + 16, width), F32),
             pltpu.VMEM((snaps, 16, depth), BF16),
             pltpu.VMEM((snaps, 16, depth), BF16),
+            pltpu.VMEM((snaps, comps_all * (cells - 16), width), F32),
             pltpu.VMEM((1, width), F32),
             pltpu.VMEM((comps_all, cells // 2, width), F32),
             pltpu.VMEM((comps_all, cells // 2, width), F32),

time: 25.3 us -> 22.7 us (0.90)
  Pallas kernels: 24.5 us -> 21.9 us
    pallas_call x1, Pallas kernels: 20.7 us -> 18.1 us  [per_device(): pl.pallas_call(functools.partial(rows_kernel, snaps, comps_all), out_shap...]
where the time goes in v4:
time: 22.7 us; the launch traced here: 22.5 us
  Pallas kernels  21.9 us (96%)
  between operations  0.64 us (3%)
    pallas_call x1, Pallas kernels, per_device(): pl.pallas_call(functools.partial(rows_kernel, snaps, comps_all), out_shap...  18.1 us
    pallas_call x1, Pallas kernels, per_device(): pl.pallas_call(functools.partial(modes_kernel, snaps, row_total), out_sha...  3.83 us

profile of v4, /device:TPU:0, one launch (start us, length us, event | category | flops | bytes accessed | tf_op | source)
XLA Modules:
  0.0 22.5 jit_solution(13445372808203644636)
XLA Ops:
  0.6 18.1 %shard_map.41 = (bf16[16,16,1536]{2,1,0:T(8,128)(2,1)}, bf16[16,16,1536]{2,1,0:T(8,128)(2,1)}, f32[2,128]{1,0:T(2,128)}) custom-call(f32[48,64,128]{2,1,0:T(8,128)} %bitcast.5, f32[1,128]{1,0:T(1,128)} %bitcast.6), custom_call_target="tpu_custom_call" | custom-call | tf_op jit(solution)/shard_map/pallas_call | solution.py:365
  18.7 3.8 %shard_map.42 = (f32[16,192,128]{2,1,0:T(8,128)}, f32[16,16]{1,0:T(8,128)}) custom-call(bf16[16,16,1536]{2,1,0:T(8,128)(2,1)} %get-tuple-element.7.high_ref, bf16[16,16,1536]{2,1,0:T(8,128)(2,1)} %get-tuple-element.8.low_ref, f32[2,128]{1,0:T(2,128)} %get-tuple-element.9.gram_ref), custom_call_target="tpu_custom_call" | custom-call | tf_op jit(solution)/shard_map/pallas_call | solution.py:398

commit v5 on v4

--- a/solution.py
+++ b/solution.py
@@ -306,8 +306,9 @@
 
     work = jnp.where(m_j == m_i + snaps, 1.0, gram)
     for k in range(snaps - 1):
-        scaled = work[k:k + 1, :] / work[k:k + 1, k:k + 1]
-        work = work - jnp.where(m_i > k, work[:, k:k + 1], 0.0) * scaled
+        column = work[:, k:k + 1]
+        factors = jnp.where(m_i[:, :1] > k, column, 0.0) * (1.0 / work[k:k + 1, k:k + 1])
+        work = work - factors * work[k:k + 1, :]
     pivots = jnp.sum(jnp.where(m_i == m_j, work, 0.0), axis=1, keepdims=True)
     work = work / jnp.sqrt(pivots)
     upper = jnp.where(m_j >= m_i, work, 0.0) * (1.0 / math.sqrt(row_total))

time: 22.7 us -> 22.7 us (level)
  no operation moved by 1% of the time
where the time goes in v5:
time: 22.7 us; the launch traced here: 22.6 us
  Pallas kernels  21.9 us (96%)
  between operations  0.64 us (3%)
    pallas_call x1, Pallas kernels, per_device(): pl.pallas_call(functools.partial(rows_kernel, snaps, comps_all), out_shap...  18.1 us
    pallas_call x1, Pallas kernels, per_device(): pl.pallas_call(functools.partial(modes_kernel, snaps, row_total), out_sha...  3.84 us

profile of v5, /device:TPU:0, one launch (start us, length us, event | category | flops | bytes accessed | tf_op | source)
XLA Modules:
  0.0 22.6 jit_solution(9477692754123051967)
XLA Ops:
  0.6 18.1 %shard_map.41 = (bf16[16,16,1536]{2,1,0:T(8,128)(2,1)}, bf16[16,16,1536]{2,1,0:T(8,128)(2,1)}, f32[2,128]{1,0:T(2,128)}) custom-call(f32[48,64,128]{2,1,0:T(8,128)} %bitcast.5, f32[1,128]{1,0:T(1,128)} %bitcast.6), custom_call_target="tpu_custom_call" | custom-call | tf_op jit(solution)/shard_map/pallas_call | solution.py:366
  18.7 3.8 %shard_map.42 = (f32[16,192,128]{2,1,0:T(8,128)}, f32[16,16]{1,0:T(8,128)}) custom-call(bf16[16,16,1536]{2,1,0:T(8,128)(2,1)} %get-tuple-element.7.high_ref, bf16[16,16,1536]{2,1,0:T(8,128)(2,1)} %get-tuple-element.8.low_ref, f32[2,128]{1,0:T(2,128)} %get-tuple-element.9.gram_ref), custom_call_target="tpu_custom_call" | custom-call | tf_op jit(solution)/shard_map/pallas_call | solution.py:399
